TPU v7x, 256 devices: a whole 4x4x8 slice. The times are simulated.
256 devices in a mesh: seq: 2 (over y_lo), ctx: 4 (over x), head: 32 (over z, y_hi, core).
Axes of the slice: x: 4, y: 4 (y_hi: 2, y_lo: 2; y = y_hi * 2 + y_lo), z: 8, core: 2. Of those that a mesh axis runs over, the one named last changes fastest.
Arguments:
- queries: bfloat16 [4, 2048, 2, 32, 128], P('ctx', ('seq', 'head')), may hold values from -8 to 8
- key_states: bfloat16 [4, 2048, 2, 32, 128], P('ctx', ('seq', 'head')), may hold values from -6 to 6
- value_states: bfloat16 [4, 2048, 2, 32, 128], P('ctx', ('seq', 'head')), may hold values from -6 to 6
- output_grad: bfloat16 [4, 2048, 2, 32, 128], P('ctx', ('seq', 'head')), may hold values from -6 to 6
Outputs:
- attention_out: bfloat16 [4, 2048, 2, 32, 128], P('ctx', ('seq', 'head'))
- query_grad: bfloat16 [4, 2048, 2, 32, 128], P('ctx', ('seq', 'head'))
- key_grad: bfloat16 [4, 2048, 2, 32, 128], P('ctx', ('seq', 'head'))
- value_grad: bfloat16 [4, 2048, 2, 32, 128], P('ctx', ('seq', 'head'))
All inputs are finite; a program needn't handle non-finite values.
Results may differ from a plain program's by a relative error of at most 0.0088.
Values may be sent and summed in bfloat16 or wider, within the bound.
A program may use at most 64 MiB of HBM per device.

v0:
```python
import jax
import jax.numpy as jnp
from jax import lax
from jax.sharding import PartitionSpec as P

H = 32


def as_sent(x):

    def short(part):
        return part.astype(jnp.bfloat16) if part.dtype == jnp.float32 else part

    return jax.tree.map(short, x)


def from_behind(block, axis, distance):
    devices = range(lax.axis_size(axis))
    route = [((i - distance) % len(devices), i) for i in devices]
    return lax.ppermute(block, axis, route)


def group_attention(query_rows, key_rows, value_rows, grad_rows):
    length, head_count, head_width = query_rows.shape
    scaling = head_width ** (-0.5)
    block_len = min(512, length)
    key_total = jnp.zeros(key_rows.shape, jnp.float32)
    value_total = jnp.zeros(key_rows.shape, jnp.float32)
    outputs = []
    query_parts = []
    for row_block in range(length // block_len):
        start = row_block * block_len
        limit = start + block_len
        q_part = query_rows[start:limit]
        g_part = grad_rows[start:limit]
        k_part = key_rows[:limit]
        v_part = value_rows[:limit]
        scores = (
            jnp.einsum("qhd,khd->hqk", q_part, k_part, preferred_element_type=jnp.float32) * scaling
        )
        causal = jnp.arange(limit)[None, :] <= start + jnp.arange(block_len)[:, None]
        scores = jnp.where(causal[None], scores, -jnp.inf)
        largest = jnp.max(scores, axis=2, keepdims=True)
        weights = jnp.exp(scores - largest)
        weights = weights / jnp.sum(weights, axis=2, keepdims=True)
        weights_low = weights.astype(jnp.bfloat16)
        attended = jnp.einsum(
            "hqk,khd->qhd", weights_low, v_part, preferred_element_type=jnp.float32
        )
        grad_probs = jnp.einsum("qhd,khd->hqk", g_part, v_part, preferred_element_type=jnp.float32)
        row_dot = jnp.transpose(jnp.sum(g_part.astype(jnp.float32) * attended, axis=2))[:, :, None]
        grad_low = (weights * (grad_probs - row_dot)).astype(jnp.bfloat16)
        query_parts.append(
            jnp.einsum("hqk,khd->qhd", grad_low, k_part, preferred_element_type=jnp.float32)
            * scaling
        )
        key_total = key_total.at[:limit].add(
            jnp.einsum("hqk,qhd->khd", grad_low, q_part, preferred_element_type=jnp.float32)
            * scaling
        )
        value_total = value_total.at[:limit].add(
            jnp.einsum("hqk,qhd->khd", weights_low, g_part, preferred_element_type=jnp.float32)
        )
        outputs.append(attended)
    return (
        jnp.concatenate(outputs, axis=0).astype(jnp.bfloat16),
        jnp.concatenate(query_parts, axis=0).astype(jnp.bfloat16),
        key_total.astype(jnp.bfloat16),
        value_total.astype(jnp.bfloat16),
    )


def shifted_flags(held_heads):
    head_ids = lax.axis_index("head") * held_heads + jnp.arange(held_heads)
    return (head_ids >= H // 2)[None, :, None]


def advance_heads(arrays):
    middle = arrays[0].shape[0] // 2
    flags = shifted_flags(arrays[0].shape[1])
    firsts = tuple((array[:middle] for array in arrays))
    arrived = jax.tree.map(
        lambda part, own: part.astype(own.dtype), from_behind(as_sent(firsts), "ctx", -1), firsts
    )
    return tuple(
        (
            jnp.where(flags, jnp.concatenate([array[middle:], later], axis=0), array)
            for array, later in zip(arrays, arrived)
        )
    )


def retreat_heads(arrays):
    middle = arrays[0].shape[0] // 2
    flags = shifted_flags(arrays[0].shape[1])
    lasts = tuple((array[middle:] for array in arrays))
    arrived = jax.tree.map(
        lambda part, own: part.astype(own.dtype), from_behind(as_sent(lasts), "ctx", 1), lasts
    )
    return tuple(
        (
            jnp.where(flags, jnp.concatenate([earlier, array[:middle]], axis=0), array)
            for array, earlier in zip(arrays, arrived)
        )
    )


def joint_in(arrays):
    tok_rows, seq_count, head_count, head_width = arrays[0].shape
    pieces = tuple(
        (array.reshape(1, tok_rows, seq_count * head_count, head_width) for array in arrays)
    )
    moved = jax.tree.map(
        lambda part, own: part.astype(own.dtype),
        lax.all_to_all(as_sent(pieces), ("seq", "head"), split_axis=2, concat_axis=0, tiled=True),
        pieces,
    )
    return tuple(
        (
            block.reshape(block.shape[0] * block.shape[1], block.shape[2], head_width)
            for block in moved
        )
    )


def joint_out(arrays, tok_rows, seq_count, head_count):
    length, held_heads, head_width = arrays[0].shape
    pieces = tuple(
        (array.reshape(length // tok_rows, tok_rows, held_heads, head_width) for array in arrays)
    )
    moved = jax.tree.map(
        lambda part, own: part.astype(own.dtype),
        lax.all_to_all(as_sent(pieces), ("seq", "head"), split_axis=0, concat_axis=2, tiled=True),
        pieces,
    )
    return tuple((block.reshape(tok_rows, seq_count, head_count, head_width) for block in moved))


def shards(queries, key_states, value_states, output_grad):
    arrays = (queries[0], key_states[0], value_states[0], output_grad[0])
    tok_rows, seq_count, head_count, head_width = arrays[0].shape
    head_side = joint_in(arrays)
    head_side = advance_heads(head_side)
    results = group_attention(head_side[0], head_side[1], head_side[2], head_side[3])
    results = retreat_heads(results)
    token_side = joint_out(results, tok_rows, seq_count, head_count)
    return (token_side[0][None], token_side[1][None], token_side[2][None], token_side[3][None])


def solution(mesh):
    in_specs = (
        P("ctx", ("seq", "head"), None, None, None),
        P("ctx", ("seq", "head"), None, None, None),
        P("ctx", ("seq", "head"), None, None, None),
        P("ctx", ("seq", "head"), None, None, None),
    )
    out_specs = (
        P("ctx", ("seq", "head"), None, None, None),
        P("ctx", ("seq", "head"), None, None, None),
        P("ctx", ("seq", "head"), None, None, None),
        P("ctx", ("seq", "head"), None, None, None),
    )
    return jax.shard_map(shards, mesh=mesh, in_specs=in_specs, out_specs=out_specs, check_vma=False)
```

profile of v0, /device:TPU:1, one launch (start us, length us, event | category | flops | bytes accessed | tf_op | source)
XLA Modules:
  0.0 272.2 jit_solution(348478472112496743)
XLA Ops:
  0.7 2.3 copy.54
  2.9 13.2 %all-to-all-start.2 = ((bf16[1,32,64,128]{3,1,0,2:T(8,128)(2,1)}), bf16[1,32,64,128]{3,1,0,2:T(8,128)(2,1)S(1)}, u32[]{:S(2)}, u32[]{:S(2)}) async-start(bf16[1,32,64,128]{3,1,0,2:T(8,128)(2,1)} %bitcast.16), calls=%async_computation.2 | async-start | bytes 1048576 | tf_op jit(solution)/shard_map/all_to_all | solution.py:115
  17.2 15.8 %all-to-all-done.2 = bf16[1,32,64,128]{3,1,0,2:T(8,128)(2,1)S(1)} async-done(((bf16[1,32,64,128]{3,1,0,2:T(8,128)(2,1)}), bf16[1,32,64,128]{3,1,0,2:T(8,128)(2,1)S(1)}, u32[]{:S(2)}, u32[]{:S(2)}) %all-to-all-start.2) | async-done | bytes 524320 | tf_op jit(solution)/shard_map/all_to_all | solution.py:115
  33.0 6.7 %all-to-all-start.1 = ((bf16[1,32,64,128]{3,1,0,2:T(8,128)(2,1)}), bf16[1,32,64,128]{3,1,0,2:T(8,128)(2,1)S(1)}, u32[]{:S(2)}, u32[]{:S(2)}) async-start(bf16[1,32,64,128]{3,1,0,2:T(8,128)(2,1)} %bitcast.8), calls=%async_computation.1 | async-start | bytes 1048576 | tf_op jit(solution)/shard_map/all_to_all | solution.py:115
  40.9 15.8 %all-to-all-done.1 = bf16[1,32,64,128]{3,1,0,2:T(8,128)(2,1)S(1)} async-done(((bf16[1,32,64,128]{3,1,0,2:T(8,128)(2,1)}), bf16[1,32,64,128]{3,1,0,2:T(8,128)(2,1)S(1)}, u32[]{:S(2)}, u32[]{:S(2)}) %all-to-all-start.1) | async-done | bytes 524320 | tf_op jit(solution)/shard_map/all_to_all | solution.py:115
  56.6 6.7 %all-to-all-start.4 = ((bf16[1,32,64,128]{3,1,0,2:T(8,128)(2,1)}), bf16[1,32,64,128]{3,1,0,2:T(8,128)(2,1)S(1)}, u32[]{:S(2)}, u32[]{:S(2)}) async-start(bf16[1,32,64,128]{3,1,0,2:T(8,128)(2,1)} %bitcast.52), calls=%async_computation.4 | async-start | bytes 1048576 | tf_op jit(solution)/shard_map/all_to_all | solution.py:115
  64.5 15.8 %all-to-all-done.4 = bf16[1,32,64,128]{3,1,0,2:T(8,128)(2,1)S(1)} async-done(((bf16[1,32,64,128]{3,1,0,2:T(8,128)(2,1)}), bf16[1,32,64,128]{3,1,0,2:T(8,128)(2,1)S(1)}, u32[]{:S(2)}, u32[]{:S(2)}) %all-to-all-start.4) | async-done | bytes 524320 | tf_op jit(solution)/shard_map/all_to_all | solution.py:115
  80.3 6.7 %all-to-all-start = ((bf16[1,32,64,128]{3,1,0,2:T(8,128)(2,1)}), bf16[1,32,64,128]{3,1,0,2:T(8,128)(2,1)S(1)}, u32[]{:S(2)}, u32[]{:S(2)}) async-start(bf16[1,32,64,128]{3,1,0,2:T(8,128)(2,1)} %bitcast), calls=%async_computation | async-start | bytes 1048576 | tf_op jit(solution)/shard_map/all_to_all | solution.py:115
  87.9 2.5 collective-permute-start.2
  99.1 4.8 %all-to-all-done = bf16[1,32,64,128]{3,1,0,2:T(8,128)(2,1)S(1)} async-done(((bf16[1,32,64,128]{3,1,0,2:T(8,128)(2,1)}), bf16[1,32,64,128]{3,1,0,2:T(8,128)(2,1)S(1)}, u32[]{:S(2)}, u32[]{:S(2)}) %all-to-all-start) | async-done | bytes 524320 | tf_op jit(solution)/shard_map/all_to_all | solution.py:115
  104.8 2.5 collective-permute-start
  119.6 2.6 fusion.24
  126.1 2.5 fusion.12
  130.3 2.0 copy.61
  133.5 2.2 fusion.67
  137.3 2.7 fusion.16
  142.8 2.0 copy.59
  146.0 3.2 %convolution_bitcast_fusion.4 = f32[512,1,128]{0,2,1:T(8,128)S(1)} fusion(bf16[2048,128]{1,0:T(8,128)(2,1)S(1)} %bitcast.256, f32[512,2048]{1,0:T(8,128)} %copy-done), kind=kOutput, calls=%fused_computation.54 | convolution fusion | flops 269484032 | bytes 4980736 | tf_op jit(solution)/shard_map/hqk,khd->qhd/dot_general | solution.py:47
  154.4 2.5 copy-done.1
  159.5 7.7 %collective-permute-done.6 = bf16[1024,1,128]{0,2,1:T(8,128)(2,1)S(1)} collective-permute-done((bf16[1024,1,128]{0,2,1:T(8,128)(2,1)S(1)}, bf16[1024,1,128]{0,2,1:T(8,128)(2,1)S(1)}, u32[]{:S(2)}, u32[]{:S(2)}) %collective-permute-start.6) | collective-permute-done | bytes 262176 | tf_op jit(solution)/shard_map/ppermute | solution.py:20
  167.1 2.3 maximum_select_fusion.6
  169.4 2.2 copy.71
  171.6 8.5 %all-to-all-start.6 = ((bf16[64,32,1,128]{3,1,2,0:T(8,128)(2,1)}), bf16[64,32,1,128]{3,1,2,0:T(8,128)(2,1)}, u32[]{:S(2)}, u32[]{:S(2)}) async-start(bf16[64,32,1,128]{3,1,2,0:T(8,128)(2,1)} %bitcast.268), calls=%async_computation.6 | async-start | bytes 1048576 | tf_op jit(solution)/shard_map/all_to_all | solution.py:133
  185.9 11.1 %all-to-all-done.6 = bf16[64,32,1,128]{3,1,2,0:T(8,128)(2,1)} async-done(((bf16[64,32,1,128]{3,1,2,0:T(8,128)(2,1)}), bf16[64,32,1,128]{3,1,2,0:T(8,128)(2,1)}, u32[]{:S(2)}, u32[]{:S(2)}) %all-to-all-start.6) | async-done | bytes 524320 | tf_op jit(solution)/shard_map/all_to_all | solution.py:133
  197.0 6.8 %all-to-all-start.7 = ((bf16[64,32,1,128]{3,1,2,0:T(8,128)(2,1)}), bf16[64,32,1,128]{3,1,2,0:T(8,128)(2,1)S(1)}, u32[]{:S(2)}, u32[]{:S(2)}) async-start(bf16[64,32,1,128]{3,1,2,0:T(8,128)(2,1)} %bitcast.102), calls=%async_computation.7 | async-start | bytes 1048576 | tf_op jit(solution)/shard_map/all_to_all | solution.py:133
  204.4 8.3 %collective-permute-done.5 = bf16[1024,1,128]{0,2,1:T(8,128)(2,1)S(1)} collective-permute-done((bf16[1024,1,128]{0,2,1:T(8,128)(2,1)S(1)}, bf16[1024,1,128]{0,2,1:T(8,128)(2,1)S(1)}, u32[]{:S(2)}, u32[]{:S(2)}) %collective-permute-start.5) | collective-permute-done | bytes 262176 | tf_op jit(solution)/shard_map/ppermute | solution.py:20
  212.6 5.6 %collective-permute-done.3 = bf16[1024,1,128]{0,2,1:T(8,128)(2,1)S(1)} collective-permute-done((bf16[1024,1,128]{0,2,1:T(8,128)(2,1)S(1)}, bf16[1024,1,128]{0,2,1:T(8,128)(2,1)S(1)}, u32[]{:S(2)}, u32[]{:S(2)}) %collective-permute-start.3) | collective-permute-done | bytes 262176 | tf_op jit(solution)/shard_map/ppermute | solution.py:20
  220.8 9.9 %all-to-all-start.3 = ((bf16[64,32,1,128]{3,1,2,0:T(8,128)(2,1)}), bf16[64,32,1,128]{3,1,2,0:T(8,128)(2,1)S(1)}, u32[]{:S(2)}, u32[]{:S(2)}) async-start(bf16[64,32,1,128]{3,1,2,0:T(8,128)(2,1)} %bitcast.48), calls=%async_computation.3 | async-start | bytes 1048576 | tf_op jit(solution)/shard_map/all_to_all | solution.py:133
  231.7 15.9 %all-to-all-done.3 = bf16[64,32,1,128]{3,1,2,0:T(8,128)(2,1)S(1)} async-done(((bf16[64,32,1,128]{3,1,2,0:T(8,128)(2,1)}), bf16[64,32,1,128]{3,1,2,0:T(8,128)(2,1)S(1)}, u32[]{:S(2)}, u32[]{:S(2)}) %all-to-all-start.3) | async-done | bytes 524320 | tf_op jit(solution)/shard_map/all_to_all | solution.py:133
  247.6 6.7 %all-to-all-start.5 = ((bf16[64,32,1,128]{3,1,2,0:T(8,128)(2,1)}), bf16[64,32,1,128]{3,1,2,0:T(8,128)(2,1)S(1)}, u32[]{:S(2)}, u32[]{:S(2)}) async-start(bf16[64,32,1,128]{3,1,2,0:T(8,128)(2,1)} %bitcast.76), calls=%async_computation.5 | async-start | bytes 1048576 | tf_op jit(solution)/shard_map/all_to_all | solution.py:133
  254.3 2.0 copy.77
  258.3 12.9 %all-to-all-done.5 = bf16[64,32,1,128]{3,1,2,0:T(8,128)(2,1)S(1)} async-done(((bf16[64,32,1,128]{3,1,2,0:T(8,128)(2,1)}), bf16[64,32,1,128]{3,1,2,0:T(8,128)(2,1)S(1)}, u32[]{:S(2)}, u32[]{:S(2)}) %all-to-all-start.5) | async-done | bytes 524320 | tf_op jit(solution)/shard_map/all_to_all | solution.py:133
  (174 shorter events, 58.4 us)
Async XLA Ops:
  0.6 15.4 %copy-start.42 = (bf16[1,32,2,32,128]{4,3,2,1,0:T(8,128)(2,1)S(1)}, bf16[1,32,2,32,128]{4,3,2,1,0:T(8,128)(2,1)}, u32[]{:S(2)}) copy-start(bf16[1,32,2,32,128]{4,3,2,1,0:T(8,128)(2,1)} %param.24) | copy-start | bytes 1572868
  0.6 39.1 %copy-start.43 = (bf16[1,32,2,32,128]{4,3,2,1,0:T(8,128)(2,1)S(1)}, bf16[1,32,2,32,128]{4,3,2,1,0:T(8,128)(2,1)}, u32[]{:S(2)}) copy-start(bf16[1,32,2,32,128]{4,3,2,1,0:T(8,128)(2,1)} %param.27) | copy-start | bytes 1572868
  2.9 30.1 %all-to-all-start.2 = ((bf16[1,32,64,128]{3,1,0,2:T(8,128)(2,1)}), bf16[1,32,64,128]{3,1,0,2:T(8,128)(2,1)S(1)}, u32[]{:S(2)}, u32[]{:S(2)}) async-start(bf16[1,32,64,128]{3,1,0,2:T(8,128)(2,1)} %bitcast.16), calls=%async_computation.2 | async-start | bytes 1048576 | tf_op jit(solution)/shard_map/all_to_all | solution.py:115
  16.1 47.3 %copy-start.44 = (bf16[1,32,2,32,128]{4,3,2,1,0:T(8,128)(2,1)S(1)}, bf16[1,32,2,32,128]{4,3,2,1,0:T(8,128)(2,1)}, u32[]{:S(2)}) copy-start(bf16[1,32,2,32,128]{4,3,2,1,0:T(8,128)(2,1)} %param.26) | copy-start | bytes 1572868
  33.0 57.5 %copy-start.4 = (bf16[1,32,64,128]{3,1,0,2:T(8,128)(2,1)}, bf16[1,32,64,128]{3,1,0,2:T(8,128)(2,1)S(1)}, u32[]{:S(2)}) copy-start(bf16[1,32,64,128]{3,1,0,2:T(8,128)(2,1)S(1)} %all-to-all-done.2) | copy-start | bytes 1572868
  33.0 23.6 %all-to-all-start.1 = ((bf16[1,32,64,128]{3,1,0,2:T(8,128)(2,1)}), bf16[1,32,64,128]{3,1,0,2:T(8,128)(2,1)S(1)}, u32[]{:S(2)}, u32[]{:S(2)}) async-start(bf16[1,32,64,128]{3,1,0,2:T(8,128)(2,1)} %bitcast.8), calls=%async_computation.1 | async-start | bytes 1048576 | tf_op jit(solution)/shard_map/all_to_all | solution.py:115
  56.6 23.6 %all-to-all-start.4 = ((bf16[1,32,64,128]{3,1,0,2:T(8,128)(2,1)}), bf16[1,32,64,128]{3,1,0,2:T(8,128)(2,1)S(1)}, u32[]{:S(2)}, u32[]{:S(2)}) async-start(bf16[1,32,64,128]{3,1,0,2:T(8,128)(2,1)} %bitcast.52), calls=%async_computation.4 | async-start | bytes 1048576 | tf_op jit(solution)/shard_map/all_to_all | solution.py:115
  80.3 23.6 %all-to-all-start = ((bf16[1,32,64,128]{3,1,0,2:T(8,128)(2,1)}), bf16[1,32,64,128]{3,1,0,2:T(8,128)(2,1)S(1)}, u32[]{:S(2)}, u32[]{:S(2)}) async-start(bf16[1,32,64,128]{3,1,0,2:T(8,128)(2,1)} %bitcast), calls=%async_computation | async-start | bytes 1048576 | tf_op jit(solution)/shard_map/all_to_all | solution.py:115
  87.9 22.1 %collective-permute-start.2 = (bf16[1024,1,128]{0,2,1:T(8,128)(2,1)}, bf16[1024,1,128]{0,2,1:T(8,128)(2,1)}, u32[]{:S(2)}, u32[]{:S(2)}) collective-permute-start(bf16[1024,1,128]{0,2,1:T(8,128)(2,1)} %copy.55), channel_id=1, source_target_pairs={{32,0},{64,32},{96,64},{0,96},{33,1},{65,33},{97,65},{1,97},{34,2}... | collective-permute-start | bytes 786440 | tf_op jit(solution)/shard_map/ppermute | solution.py:20
  91.7 19.4 %collective-permute-start.1 = (bf16[1024,1,128]{0,2,1:T(8,128)(2,1)}, bf16[1024,1,128]{0,2,1:T(8,128)(2,1)}, u32[]{:S(2)}, u32[]{:S(2)}) collective-permute-start(bf16[1024,1,128]{0,2,1:T(8,128)(2,1)} %copy.51), channel_id=1, source_target_pairs={{32,0},{64,32},{96,64},{0,96},{33,1},{65,33},{97,65},{1,97},{34,2}... | collective-permute-start | bytes 786440 | tf_op jit(solution)/shard_map/ppermute | solution.py:20
  95.2 20.6 %collective-permute-start.4 = (bf16[1024,1,128]{0,2,1:T(8,128)(2,1)}, bf16[1024,1,128]{0,2,1:T(8,128)(2,1)}, u32[]{:S(2)}, u32[]{:S(2)}) collective-permute-start(bf16[1024,1,128]{0,2,1:T(8,128)(2,1)} %copy.65), channel_id=1, source_target_pairs={{32,0},{64,32},{96,64},{0,96},{33,1},{65,33},{97,65},{1,97},{34,2}... | collective-permute-start | bytes 786440 | tf_op jit(solution)/shard_map/ppermute | solution.py:20
  103.9 7.2 %copy-start.5 = (bf16[1,32,64,128]{3,1,0,2:T(8,128)(2,1)}, bf16[1,32,64,128]{3,1,0,2:T(8,128)(2,1)S(1)}, u32[]{:S(2)}) copy-start(bf16[1,32,64,128]{3,1,0,2:T(8,128)(2,1)S(1)} %all-to-all-done) | copy-start | bytes 1572868
  104.8 17.4 %collective-permute-start = (bf16[1024,1,128]{0,2,1:T(8,128)(2,1)}, bf16[1024,1,128]{0,2,1:T(8,128)(2,1)}, u32[]{:S(2)}, u32[]{:S(2)}) collective-permute-start(bf16[1024,1,128]{0,2,1:T(8,128)(2,1)} %copy.47), channel_id=1, source_target_pairs={{32,0},{64,32},{96,64},{0,96},{33,1},{65,33},{97,65},{1,97},{34,2}... | collective-permute-start | bytes 786440 | tf_op jit(solution)/shard_map/ppermute | solution.py:20
  113.4 9.9 %copy-start.25 = (f32[512,1024]{1,0:T(8,128)}, f32[512,1024]{1,0:T(8,128)S(1)}, u32[]{:S(2)}) copy-start(f32[512,1024]{1,0:T(8,128)S(1)} %get-tuple-element.149) | copy-start | bytes 6291460
  117.6 8.4 %copy-start.20 = (bf16[2048,1,128]{0,2,1:T(8,128)(2,1)}, bf16[2048,1,128]{0,2,1:T(8,128)(2,1)S(1)}, u32[]{:S(2)}) copy-start(bf16[2048,1,128]{0,2,1:T(8,128)(2,1)S(1)} %maximum_select_fusion.4) | copy-start | bytes 1572868
  141.0 18.4 %collective-permute-start.7 = (bf16[1024,1,128]{0,2,1:T(8,128)(2,1)}, bf16[1024,1,128]{0,2,1:T(8,128)(2,1)}, u32[]{:S(2)}, u32[]{:S(2)}) collective-permute-start(bf16[1024,1,128]{0,2,1:T(8,128)(2,1)} %get-tuple-element.128), channel_id=1, source_target_pairs={{96,0},{0,32},{32,64},{64,96},{97,1},{1,33},{33,65},{65,97},{98,2}... | collective-permute-start | bytes 786440 | tf_op jit(solution)/shard_map/ppermute | solution.py:20
  146.0 4.2 %copy-start.11 = (f32[512,512]{0,1:T(8,128)S(1)}, f32[512,512]{0,1:T(8,128)}, u32[]{:S(2)}) copy-start(f32[512,512]{0,1:T(8,128)} %copy-done.10) | copy-start | bytes 3145732
  153.7 4.1 %copy-start.12 = (bf16[512,1024]{1,0:T(8,128)(2,1)}, bf16[512,1024]{1,0:T(8,128)(2,1)S(1)}, u32[]{:S(2)}) copy-start(bf16[512,1024]{1,0:T(8,128)(2,1)S(1)} %multiply_convert_fusion.1) | copy-start | bytes 3145732
  158.6 8.5 %copy-start.9 = (bf16[2048,1,128]{0,2,1:T(8,128)(2,1)S(1)}, bf16[2048,1,128]{0,2,1:T(8,128)(2,1)}, u32[]{:S(2)}) copy-start(bf16[2048,1,128]{0,2,1:T(8,128)(2,1)} %copy-done.8) | copy-start | bytes 1572868
  158.6 8.5 %copy-start.41 = (bf16[1024,1,128]{0,2,1:T(8,128)(2,1)S(1)}, bf16[1024,1,128]{0,2,1:T(8,128)(2,1)}, u32[]{:S(2)}) copy-start(bf16[1024,1,128]{0,2,1:T(8,128)(2,1)} %get-tuple-element.129) | copy-start | bytes 786436
  159.2 7.9 %collective-permute-start.6 = (bf16[1024,1,128]{0,2,1:T(8,128)(2,1)S(1)}, bf16[1024,1,128]{0,2,1:T(8,128)(2,1)S(1)}, u32[]{:S(2)}, u32[]{:S(2)}) collective-permute-start(bf16[1024,1,128]{0,2,1:T(8,128)(2,1)S(1)} %get-tuple-element.130), channel_id=1, source_target_pairs={{96,0},{0,32},{32,64},{64,96},{97,1},{1,33},{33,65},{65,97},{98,2}... | collective-permute-start | bytes 786440 | tf_op jit(solution)/shard_map/ppermute | solution.py:20
  169.4 12.3 %copy-start.13 = (bf16[512,1024]{1,0:T(8,128)(2,1)S(1)}, bf16[512,1024]{1,0:T(8,128)(2,1)}, u32[]{:S(2)}) copy-start(bf16[512,1024]{1,0:T(8,128)(2,1)} %copy-done.12) | copy-start | bytes 3145732
  171.6 25.4 %all-to-all-start.6 = ((bf16[64,32,1,128]{3,1,2,0:T(8,128)(2,1)}), bf16[64,32,1,128]{3,1,2,0:T(8,128)(2,1)}, u32[]{:S(2)}, u32[]{:S(2)}) async-start(bf16[64,32,1,128]{3,1,2,0:T(8,128)(2,1)} %bitcast.268), calls=%async_computation.6 | async-start | bytes 1048576 | tf_op jit(solution)/shard_map/all_to_all | solution.py:133
  184.7 19.3 %copy-start.15 = (f32[512,1,128]{0,2,1:T(8,128)S(1)}, f32[512,1,128]{0,2,1:T(8,128)}, u32[]{:S(2)}) copy-start(f32[512,1,128]{0,2,1:T(8,128)} %convolution_bitcast_fusion.7) | copy-start | bytes 786436
  184.7 19.3 %copy-start.23 = (f32[512,1,128]{0,2,1:T(8,128)S(1)}, f32[512,1,128]{0,2,1:T(8,128)}, u32[]{:S(2)}) copy-start(f32[512,1,128]{0,2,1:T(8,128)} %convolution_bitcast_fusion.6) | copy-start | bytes 786436
  184.7 19.3 %copy-start.34 = (bf16[512,1,128]{0,2,1:T(8,128)(2,1)S(1)}, bf16[512,1,128]{0,2,1:T(8,128)(2,1)}, u32[]{:S(2)}) copy-start(bf16[512,1,128]{0,2,1:T(8,128)(2,1)} %get-tuple-element.152) | copy-start | bytes 393220
  197.0 21.2 %copy-start.36 = (bf16[512,1,128]{0,2,1:T(8,128)(2,1)S(1)}, bf16[512,1,128]{0,2,1:T(8,128)(2,1)}, u32[]{:S(2)}) copy-start(bf16[512,1,128]{0,2,1:T(8,128)(2,1)} %copy-done.35) | copy-start | bytes 393220
  197.0 23.8 %all-to-all-start.7 = ((bf16[64,32,1,128]{3,1,2,0:T(8,128)(2,1)}), bf16[64,32,1,128]{3,1,2,0:T(8,128)(2,1)S(1)}, u32[]{:S(2)}, u32[]{:S(2)}) async-start(bf16[64,32,1,128]{3,1,2,0:T(8,128)(2,1)} %bitcast.102), calls=%async_computation.7 | async-start | bytes 1048576 | tf_op jit(solution)/shard_map/all_to_all | solution.py:133
  203.9 8.7 %collective-permute-start.5 = (bf16[1024,1,128]{0,2,1:T(8,128)(2,1)S(1)}, bf16[1024,1,128]{0,2,1:T(8,128)(2,1)S(1)}, u32[]{:S(2)}, u32[]{:S(2)}) collective-permute-start(bf16[1024,1,128]{0,2,1:T(8,128)(2,1)S(1)} %get-tuple-element.132), channel_id=1, source_target_pairs={{96,0},{0,32},{32,64},{64,96},{97,1},{1,33},{33,65},{65,97},{98,2}... | collective-permute-start | bytes 786440 | tf_op jit(solution)/shard_map/ppermute | solution.py:20
  204.1 14.1 %collective-permute-start.3 = (bf16[1024,1,128]{0,2,1:T(8,128)(2,1)S(1)}, bf16[1024,1,128]{0,2,1:T(8,128)(2,1)S(1)}, u32[]{:S(2)}, u32[]{:S(2)}) collective-permute-start(bf16[1024,1,128]{0,2,1:T(8,128)(2,1)S(1)} %get-tuple-element.136), channel_id=1, source_target_pairs={{96,0},{0,32},{32,64},{64,96},{97,1},{1,33},{33,65},{65,97},{98,2}... | collective-permute-start | bytes 786440 | tf_op jit(solution)/shard_map/ppermute | solution.py:20
  220.8 26.8 %all-to-all-start.3 = ((bf16[64,32,1,128]{3,1,2,0:T(8,128)(2,1)}), bf16[64,32,1,128]{3,1,2,0:T(8,128)(2,1)S(1)}, u32[]{:S(2)}, u32[]{:S(2)}) async-start(bf16[64,32,1,128]{3,1,2,0:T(8,128)(2,1)} %bitcast.48), calls=%async_computation.3 | async-start | bytes 1048576 | tf_op jit(solution)/shard_map/all_to_all | solution.py:133
  247.6 23.6 %all-to-all-start.5 = ((bf16[64,32,1,128]{3,1,2,0:T(8,128)(2,1)}), bf16[64,32,1,128]{3,1,2,0:T(8,128)(2,1)S(1)}, u32[]{:S(2)}, u32[]{:S(2)}) async-start(bf16[64,32,1,128]{3,1,2,0:T(8,128)(2,1)} %bitcast.76), calls=%async_computation.5 | async-start | bytes 1048576 | tf_op jit(solution)/shard_map/all_to_all | solution.py:133
  (29 other events, 69.6 us)
where the time goes:
time: 274 us; the launch traced here: 272 us
  waiting for transfers between devices  115 us (42%)
  starting transfers between devices  71.6 us (26%)
  local copies, waits for them, and re-layouts  40.2 us (15%)
  matrix products  27.5 us (10%)
  other arithmetic  16.6 us (6%)
    all_to_all x4, waiting for transfers between devices, joint_in(): lax.all_to_all(as_sent(pieces), ('seq', 'head'), split_axis=2, concat_axi...  52.1 us
    all_to_all x4, waiting for transfers between devices, joint_out(): lax.all_to_all(as_sent(pieces), ('seq', 'head'), split_axis=0, concat_axi...  41.2 us
    all_to_all x4, starting transfers between devices, joint_in(): lax.all_to_all(as_sent(pieces), ('seq', 'head'), split_axis=2, concat_axi...  33.3 us
    all_to_all x4, starting transfers between devices, joint_out(): lax.all_to_all(as_sent(pieces), ('seq', 'head'), split_axis=0, concat_axi...  32 us
    ppermute x8, waiting for transfers between devices, from_behind(): return lax.ppermute(block, axis, route)  21.5 us
    unnamed x98, local copies, waits for them, and re-layouts  16.3 us
    concatenate x8, local copies, waits for them, and re-layouts, advance_heads(): jnp.concatenate([array[middle:], later], axis=0)  8.7 us
    dot_general x4, matrix products, group_attention(): jnp.einsum('hqk,qhd->khd', weights_low, g_part, preferred_element_type=jn...  8.08 us
  transfers between devices with their start and end apart: 16, of which 11 were waited for; matrix products, arithmetic and copies ran while one was open for 19% of the time, Pallas kernels for 0%

commit v1 on v0

v1 whole, which is shorter than its diff:
```python
import functools
import math

import jax
import jax.numpy as jnp
from jax import lax
from jax.experimental import pallas as pl
from jax.experimental.pallas import tpu as pltpu
from jax.sharding import PartitionSpec as P

H = 32
T = 2048
D = 128
BLOCKS = 64
ROWS = T // BLOCKS
TB = 256
NB = T // TB
SCALE = D**-0.5
EXP2_SCALE = SCALE * math.log2(math.e)
NT = (((1,), (1,)), ((), ()))
NN = (((1,), (0,)), ((), ()))
MESH = pl.DeviceIdType.MESH
IN_GROUPS = ((0, 2), (2, 1), (3, 1))
OUT_GROUPS = ((0, 1), (1, 1), (2, 2))


def dot(a, b, dims=NN):
    return lax.dot_general(a, b, dims, preferred_element_type=jnp.float32)


def tile(i, n=1):
    return pl.ds(i * TB, n * TB)


def rows(block):
    return pl.ds(pl.multiple_of(block * ROWS, ROWS), ROWS)


def softmax_weights(q, k, scores, weights):
    for i in range(NB):
        q_tile = q[tile(i)]
        top = None
        for j in range(i + 1):
            s = dot(k[tile(j)], q_tile, NT)
            if j == i:
                key_pos = lax.broadcasted_iota(jnp.int32, (TB, TB), 0)
                query_pos = lax.broadcasted_iota(jnp.int32, (TB, TB), 1)
                s = jnp.where(key_pos <= query_pos, s, -jnp.inf)
            scores[tile(j)] = s
            part = jnp.max(s, axis=0, keepdims=True)
            top = part if top is None else jnp.maximum(top, part)
        shift = top * EXP2_SCALE
        total = None
        for j in range(i + 1):
            e = jnp.exp2(scores[tile(j)] * EXP2_SCALE - shift)
            scores[tile(j)] = e
            part = jnp.sum(e, axis=0, keepdims=True)
            total = part if total is None else total + part
        inverse = 1.0 / total
        for j in range(i + 1):
            weights[tile(j), tile(i)] = (scores[tile(j)] * inverse).astype(jnp.bfloat16)


def attended(v_t, weights, out, out_wide):
    for i in range(NB):
        o = dot(v_t[:, 0 : (i + 1) * TB], weights[0 : (i + 1) * TB, tile(i)]).T
        out_wide[tile(i)] = o
        out[tile(i)] = o.astype(jnp.bfloat16)


def value_grads(weights, g, dv):
    for j in range(NB):
        n = NB - j
        dv[tile(j)] = dot(weights[tile(j), tile(j, n)], g[tile(j, n)]).astype(jnp.bfloat16)


def row_dots(g, out_wide, row_dot):
    ones = jnp.ones((8, D), jnp.bfloat16)
    for i in range(NB):
        x = g[tile(i)].astype(jnp.float32) * out_wide[tile(i)]
        high = x.astype(jnp.bfloat16)
        low = (x - high.astype(jnp.float32)).astype(jnp.bfloat16)
        row_dot[:, tile(i)] = dot(ones, high, NT) + dot(ones, low, NT)


def score_grads(weights, q, k_t, v, g, row_dot, ds, dq, dk):
    for i in range(NB):
        r = row_dot[0:1, tile(i)]
        for j in range(i + 1):
            dp = dot(v[tile(j)], g[tile(i)], NT)
            w = weights[tile(j), tile(i)].astype(jnp.float32)
            ds[tile(j), tile(i)] = (w * (dp - r)).astype(jnp.bfloat16)
        grad = dot(k_t[:, 0 : (i + 1) * TB], ds[0 : (i + 1) * TB, tile(i)])
        dq[tile(i)] = (grad * SCALE).T.astype(jnp.bfloat16)
    for j in range(NB):
        n = NB - j
        dk[tile(j)] = (dot(ds[tile(j), tile(j, n)], q[tile(j, n)]) * SCALE).astype(jnp.bfloat16)


def kernel(
    q_in, k_in, v_in, g_in, o_out, dq_out, dk_out, dv_out,
    held, sent, items, made, given,
    scores, weights, ds, v_t, k_t, out_wide, row_dot,
    load_sem, store_sem, in_send, in_recv, out_send, out_recv, own_send,
):
    seq = lax.axis_index("seq")
    ctx = lax.axis_index("ctx")
    head = lax.axis_index("head")
    me = seq * 32 + head
    z = head // 4
    y = ((head // 2) % 2) * 2 + seq
    core = head % 2
    shifted_me = head >= H // 2
    local = jnp.logical_or(jnp.logical_not(shifted_me), seq == 1)

    def partner(t):
        e = t // 8
        z2 = (z + 3 * t) % 8
        y2 = (y + e) % 4
        core2 = (core + e // 4) % 2
        return y2 % 2, z2 * 4 + (y2 // 2) * 2 + core2

    def item_at(t):
        seq2, head2 = partner(t)
        shifted = (head2 >= H // 2).astype(jnp.int32)
        plane = (ctx + 4 - shifted * (1 - seq)) % 4
        return seq2, head2, plane, (me + 32 * shifted) % BLOCKS

    def owner_at(t):
        seq2, head2 = partner(t)
        shifted = shifted_me.astype(jnp.int32)
        plane = (ctx + shifted * (1 - seq2)) % 4
        return seq2, head2, plane, (seq2 * 32 + head2 + 32 * shifted) % BLOCKS

    inputs = (q_in, k_in, v_in, g_in)
    loads = [
        pltpu.make_async_copy(inputs[a].at[0], held.at[a], load_sem.at[a]) for a in range(4)
    ]
    for load in loads:
        load.start()

    barrier = pltpu.get_barrier_semaphore()

    def greet(t, _):
        seq2, head2, plane, _ = owner_at(t)
        pl.semaphore_signal(barrier, inc=1, device_id=(seq2, plane, head2), device_id_type=MESH)
        return _

    lax.fori_loop(1, BLOCKS, greet, 0)

    @pl.when(jnp.logical_not(local))
    def _():
        greet(0, 0)

    def by_head(a):
        loads[a].wait()
        x = held[a].reshape(ROWS, BLOCKS, D)
        sent[a] = jnp.swapaxes(x, 0, 1).reshape(T, D)

    def send_in(n):
        first, count = IN_GROUPS[n]
        slots = pl.ds(first, count)

        def copy(t, send_sem):
            seq2, head2, plane, place = item_at(t)
            return pltpu.make_async_remote_copy(
                src_ref=sent.at[slots, rows(seq2 * 32 + head2)],
                dst_ref=items.at[slots, rows(place)],
                send_sem=send_sem,
                recv_sem=in_recv.at[n],
                device_id=(seq2, plane, head2),
                device_id_type=MESH,
            )

        @pl.when(local)
        def _():
            place = (me + 32 * shifted_me.astype(jnp.int32)) % BLOCKS
            pltpu.make_async_copy(
                sent.at[slots, rows(me)], items.at[slots, rows(place)], in_recv.at[n]
            ).start()

        @pl.when(jnp.logical_not(local))
        def _():
            copy(0, own_send.at[n]).start()

        def step(t, _):
            copy(t, in_send.at[n]).start()
            return _

        lax.fori_loop(1, BLOCKS, step, 0)

    def send_out(n):
        first, count = OUT_GROUPS[n]
        slots = pl.ds(first, count)

        def copy(t, send_sem):
            seq2, head2, plane, place = owner_at(t)
            return pltpu.make_async_remote_copy(
                src_ref=made.at[slots, rows(place)],
                dst_ref=given.at[slots, rows(me)],
                send_sem=send_sem,
                recv_sem=out_recv.at[n],
                device_id=(seq2, plane, head2),
                device_id_type=MESH,
            )

        @pl.when(local)
        def _():
            place = (me + 32 * shifted_me.astype(jnp.int32)) % BLOCKS
            pltpu.make_async_copy(
                made.at[slots, rows(place)], given.at[slots, rows(me)], out_recv.at[n]
            ).start()

        @pl.when(jnp.logical_not(local))
        def _():
            copy(0, own_send.at[3 + n]).start()

        def step(t, _):
            copy(t, out_send.at[n]).start()
            return _

        lax.fori_loop(1, BLOCKS, step, 0)

    def arrived(buffer, groups, sems, n):
        first, count = groups[n]
        whole = buffer.at[pl.ds(first, count)]
        pltpu.make_async_copy(whole, whole, sems.at[n]).wait()

    def left(buffer, groups, sems, n, own):
        first, count = groups[n]
        most = buffer.at[pl.ds(first, count), pl.ds(0, T - ROWS)]
        pltpu.make_async_copy(most, most, sems.at[n]).wait()

        @pl.when(jnp.logical_not(local))
        def _():
            one = buffer.at[pl.ds(first, count), pl.ds(0, ROWS)]
            pltpu.make_async_copy(one, one, own_send.at[own]).wait()

    by_head(0)
    by_head(1)
    pl.semaphore_wait(barrier, BLOCKS - local.astype(jnp.int32))
    send_in(0)
    by_head(2)
    send_in(1)
    by_head(3)
    send_in(2)

    q, k, v, g = (items.at[a] for a in range(4))
    arrived(items, IN_GROUPS, in_recv, 0)
    softmax_weights(q, k, scores, weights)
    k_t[...] = k[...].T
    arrived(items, IN_GROUPS, in_recv, 1)
    v_t[...] = v[...].T
    attended(v_t, weights, made.at[0], out_wide)
    send_out(0)
    arrived(items, IN_GROUPS, in_recv, 2)
    value_grads(weights, g, made.at[1])
    send_out(1)
    row_dots(g, out_wide, row_dot)
    score_grads(weights, q, k_t, v, g, row_dot, ds, made.at[2], made.at[3])
    send_out(2)

    for n in range(3):
        left(sent, IN_GROUPS, in_send, n, n)

    outputs = (o_out, dv_out, dq_out, dk_out)
    stores = []
    for n, (first, count) in enumerate(OUT_GROUPS):
        arrived(given, OUT_GROUPS, out_recv, n)
        for a in range(first, first + count):
            x = given[a].reshape(BLOCKS, ROWS, D)
            held[a] = jnp.swapaxes(x, 0, 1).reshape(ROWS, 2, H, D)
            store = pltpu.make_async_copy(held.at[a], outputs[a].at[0], store_sem.at[a])
            store.start()
            stores.append(store)
    for n in range(3):
        left(made, OUT_GROUPS, out_send, n, 3 + n)
    for store in stores:
        store.wait()


def shards(queries, key_states, value_states, output_grad):
    any_space = pl.BlockSpec(memory_space=pl.ANY)
    block = jax.ShapeDtypeStruct(queries.shape, jnp.bfloat16)
    low, wide = jnp.bfloat16, jnp.float32
    results = pl.pallas_call(
        kernel,
        out_shape=[block] * 4,
        in_specs=[any_space] * 4,
        out_specs=[any_space] * 4,
        scratch_shapes=[
            pltpu.VMEM((4, ROWS, 2, H, D), low),
            pltpu.VMEM((4, T, D), low),
            pltpu.VMEM((4, T, D), low),
            pltpu.VMEM((4, T, D), low),
            pltpu.VMEM((4, T, D), low),
            pltpu.VMEM((T, TB), wide),
            pltpu.VMEM((T, T), low),
            pltpu.VMEM((T, T), low),
            pltpu.VMEM((D, T), low),
            pltpu.VMEM((D, T), low),
            pltpu.VMEM((T, D), wide),
            pltpu.VMEM((8, T), wide),
            pltpu.SemaphoreType.DMA((4,)),
            pltpu.SemaphoreType.DMA((4,)),
            pltpu.SemaphoreType.DMA((3,)),
            pltpu.SemaphoreType.DMA((3,)),
            pltpu.SemaphoreType.DMA((3,)),
            pltpu.SemaphoreType.DMA((3,)),
            pltpu.SemaphoreType.DMA((6,)),
        ],
        compiler_params=pltpu.CompilerParams(
            collective_id=0, has_side_effects=True, vmem_limit_bytes=56 << 20
        ),
        cost_estimate=pl.CostEstimate(
            flops=12 * T * T * D // 2, bytes_accessed=16 * T * D, transcendentals=T * T // 2
        ),
        name="shifted_attention",
    )(queries, key_states, value_states, output_grad)
    return tuple(results)


def solution(mesh):
    spec = P("ctx", ("seq", "head"), None, None, None)
    return jax.shard_map(
        shards, mesh=mesh, in_specs=(spec,) * 4, out_specs=(spec,) * 4, check_vma=False
    )
```

time: 274 us -> 114 us (0.42)
  waiting for transfers between devices: 115 us -> 0 us
  Pallas kernels: 0 us -> 108 us
  starting transfers between devices: 71.6 us -> 0 us
  local copies, waits for them, and re-layouts: 40.2 us -> 5.18 us
  matrix products: 27.5 us -> 0 us
  other arithmetic: 16.6 us -> 0 us
    pallas_call x0 -> x1, Pallas kernels: none -> 108 us  [shards(): pl.pallas_call(kernel, out_shape=[block] * 4, in_specs=[any_space] * 4, o...]
    all_to_all x8 -> x0, waiting for transfers between devices: 93.2 us -> none  [the longest x4 52.1 us: joint_in(): lax.all_to_all(as_sent(pieces), ('seq', 'head'), split_axis=2, concat_axi...]
    all_to_all x8 -> x0, starting transfers between devices: 65.2 us -> none  [the longest x4 33.3 us: joint_in(): lax.all_to_all(as_sent(pieces), ('seq', 'head'), split_axis=2, concat_axi...]
    dot_general x24 -> x0, matrix products: 27.5 us -> none  [the longest x4 8.08 us: group_attention(): jnp.einsum('hqk,qhd->khd', weights_low, g_part, preferred_element_type=jn...]
    ppermute x8 -> x0, waiting for transfers between devices: 21.5 us -> none  [from_behind(): return lax.ppermute(block, axis, route)]
    unnamed x98 -> x10, local copies, waits for them, and re-layouts: 16.3 us -> 5.18 us
    select_n x8 -> x0, other arithmetic: 9.3 us -> none  [the longest x6 6.7 us: advance_heads(): jnp.where(flags, jnp.concatenate([array[middle:], later], axis=0), array)]
    concatenate x8 -> x0, local copies, waits for them, and re-layouts: 8.7 us -> none  [advance_heads(): jnp.concatenate([array[middle:], later], axis=0)]
  transfers between devices with their start and end apart: 16 -> 0, of which waited for: 11 -> 0; matrix products, arithmetic and copies ran while one was open for 19% -> 0% of each run, Pallas kernels for 0% -> 0%
where the time goes in v1:
time: 114 us
  Pallas kernels  108 us (95%)
  local copies, waits for them, and re-layouts  5.18 us (5%)
    pallas_call x1, Pallas kernels, shards(): pl.pallas_call(kernel, out_shape=[block] * 4, in_specs=[any_space] * 4, o...  108 us
    unnamed x10, local copies, waits for them, and re-layouts  5.18 us

profile of v1, /device:TPU:1, one launch (start us, length us, event | category | flops | bytes accessed | tf_op | source)
XLA Modules:
  0.0 114.2 jit_solution(3573529138171156870)
XLA Ops:
  0.6 108.4 %shifted_attention.1 = (bf16[1,32,2,32,128]{4,3,2,1,0:T(8,128)(2,1)}, bf16[1,32,2,32,128]{4,3,2,1,0:T(8,128)(2,1)}, bf16[1,32,2,32,128]{4,3,2,1,0:T(8,128)(2,1)}, bf16[1,32,2,32,128]{4,3,2,1,0:T(8,128)(2,1)}) custom-call(bf16[1,32,2,32,128]{4,3,2,1,0:T(8,128)(2,1)} %q_in.1, bf16[1,32,2,32,128]{4,3,2,1,0:T(8,128)(2,1)} %k_in.1, ...), custom_call_target="tpu_custom_call" | custom-call | flops 3221225472 | bytes 4194304 | tf_op jit(solution)/shard_map/shifted_attention/pallas_call | solution.py:286
  109.0 0.0 copy-start.2
  109.0 1.9 %copy.12 = bf16[1,32,2,32,128]{4,3,2,1,0:T(8,128)(2,1)} copy(bf16[1,32,2,32,128]{4,3,2,1,0:T(8,128)(2,1)} %get-tuple-element.8) | data formatting | bytes 1048576
  111.0 0.0 copy-done.2
  111.0 0.0 copy-start.1
  111.0 0.8 copy.13
  111.8 0.4 copy-done.1
  112.2 0.0 copy-start
  112.2 0.8 copy.14
  113.0 0.4 copy-done
  113.4 0.8 copy.15
Async XLA Ops:
  109.0 1.9 %copy-start.2 = (bf16[1,32,2,32,128]{4,3,2,1,0:T(8,128)(2,1)S(1)}, bf16[1,32,2,32,128]{4,3,2,1,0:T(8,128)(2,1)}, u32[]{:S(2)}) copy-start(bf16[1,32,2,32,128]{4,3,2,1,0:T(8,128)(2,1)} %get-tuple-element.9) | copy-start | bytes 1572868
  111.0 1.2 %copy-start.1 = (bf16[1,32,2,32,128]{4,3,2,1,0:T(8,128)(2,1)S(1)}, bf16[1,32,2,32,128]{4,3,2,1,0:T(8,128)(2,1)}, u32[]{:S(2)}) copy-start(bf16[1,32,2,32,128]{4,3,2,1,0:T(8,128)(2,1)} %get-tuple-element.10) | copy-start | bytes 1572868
  112.2 1.2 %copy-start = (bf16[1,32,2,32,128]{4,3,2,1,0:T(8,128)(2,1)S(1)}, bf16[1,32,2,32,128]{4,3,2,1,0:T(8,128)(2,1)}, u32[]{:S(2)}) copy-start(bf16[1,32,2,32,128]{4,3,2,1,0:T(8,128)(2,1)} %get-tuple-element.11) | copy-start | bytes 1572868

commit v2 on v1

--- a/solution.py
+++ b/solution.py
@@ -264,30 +264,34 @@
         left(sent, IN_GROUPS, in_send, n, n)
 
     outputs = (o_out, dv_out, dq_out, dk_out)
-    stores = []
     for n, (first, count) in enumerate(OUT_GROUPS):
         arrived(given, OUT_GROUPS, out_recv, n)
         for a in range(first, first + count):
             x = given[a].reshape(BLOCKS, ROWS, D)
-            held[a] = jnp.swapaxes(x, 0, 1).reshape(ROWS, 2, H, D)
-            store = pltpu.make_async_copy(held.at[a], outputs[a].at[0], store_sem.at[a])
-            store.start()
-            stores.append(store)
+            outputs[a][0] = jnp.swapaxes(x, 0, 1).reshape(ROWS, 2, H, D)
     for n in range(3):
         left(made, OUT_GROUPS, out_send, n, 3 + n)
-    for store in stores:
-        store.wait()
+
+
+def store_results(*refs):
+    sems = refs[8]
+    copies = [pltpu.make_async_copy(refs[a], refs[4 + a], sems.at[a]) for a in range(4)]
+    for copy in copies:
+        copy.start()
+    for copy in copies:
+        copy.wait()
 
 
 def shards(queries, key_states, value_states, output_grad):
-    any_space = pl.BlockSpec(memory_space=pl.ANY)
+    in_vmem = pl.BlockSpec(memory_space=pltpu.VMEM)
+    in_hbm = pl.BlockSpec(memory_space=pltpu.HBM)
     block = jax.ShapeDtypeStruct(queries.shape, jnp.bfloat16)
     low, wide = jnp.bfloat16, jnp.float32
     results = pl.pallas_call(
         kernel,
-        out_shape=[block] * 4,
-        in_specs=[any_space] * 4,
-        out_specs=[any_space] * 4,
+        out_shape=[pltpu.VMEM(queries.shape, low)] * 4,
+        in_specs=[in_hbm] * 4,
+        out_specs=[in_vmem] * 4,
         scratch_shapes=[
             pltpu.VMEM((4, ROWS, 2, H, D), low),
             pltpu.VMEM((4, T, D), low),
@@ -310,14 +314,27 @@
             pltpu.SemaphoreType.DMA((6,)),
         ],
         compiler_params=pltpu.CompilerParams(
-            collective_id=0, has_side_effects=True, vmem_limit_bytes=56 << 20
+            collective_id=0, has_side_effects=True, vmem_limit_bytes=36 << 20
         ),
         cost_estimate=pl.CostEstimate(
             flops=12 * T * T * D // 2, bytes_accessed=16 * T * D, transcendentals=T * T // 2
         ),
         name="shifted_attention",
-    )(queries, key_states, value_states, output_grad)
-    return tuple(results)
+    )(*[
+        pltpu.with_memory_space_constraint(x, pltpu.HBM)
+        for x in (queries, key_states, value_states, output_grad)
+    ])
+    return tuple(
+        pl.pallas_call(
+            store_results,
+            out_shape=[block] * 4,
+            in_specs=[in_vmem] * 4,
+            out_specs=[in_hbm] * 4,
+            scratch_shapes=[pltpu.SemaphoreType.DMA((4,))],
+            compiler_params=pltpu.CompilerParams(vmem_limit_bytes=4 << 20),
+            name="store_results",
+        )(*[pltpu.with_memory_space_constraint(x, pltpu.VMEM) for x in results])
+    )
 
 
 def solution(mesh):

time: 114 us -> 110 us (0.965)
  local copies, waits for them, and re-layouts: 5.18 us -> 0 us
    unnamed x10 -> x0, local copies, waits for them, and re-layouts: 5.18 us -> none
    pallas_call x1 -> x2, Pallas kernels: 108 us -> 109 us  [the longest x1 108 us: shards(): pl.pallas_call(kernel, out_shape=[pltpu.VMEM(queries.shape, low)] * 4, in...]
where the time goes in v2:
time: 110 us
  Pallas kernels  109 us (99%)
    pallas_call x1, Pallas kernels, shards(): pl.pallas_call(kernel, out_shape=[pltpu.VMEM(queries.shape, low)] * 4, in...  108 us

profile of v2, /device:TPU:1, one launch (start us, length us, event | category | flops | bytes accessed | tf_op | source)
XLA Modules:
  0.0 109.6 jit_solution(14815683443467511476)
XLA Ops:
  0.6 107.6 %shifted_attention.1 = (bf16[1,32,2,32,128]{4,3,2,1,0:T(8,128)(2,1)S(1)}, bf16[1,32,2,32,128]{4,3,2,1,0:T(8,128)(2,1)S(1)}, bf16[1,32,2,32,128]{4,3,2,1,0:T(8,128)(2,1)S(1)}, bf16[1,32,2,32,128]{4,3,2,1,0:T(8,128)(2,1)S(1)}) custom-call(bf16[1,32,2,32,128]{4,3,2,1,0:T(8,128)(2,1)} %q_in.1, bf16[1,32,2,32,128]{4,3,2,1,0:T(8,128)(2,1)} %k_in.1, ...), custom_call_target="tpu_custom_call" | custom-call | flops 3221225472 | bytes 4194304 | tf_op jit(solution)/shard_map/shifted_attention/pallas_call | solution.py:290
  108.2 1.3 %store_results.1 = (bf16[1,32,2,32,128]{4,3,2,1,0:T(8,128)(2,1)}, bf16[1,32,2,32,128]{4,3,2,1,0:T(8,128)(2,1)}, bf16[1,32,2,32,128]{4,3,2,1,0:T(8,128)(2,1)}, bf16[1,32,2,32,128]{4,3,2,1,0:T(8,128)(2,1)}) custom-call(bf16[1,32,2,32,128]{4,3,2,1,0:T(8,128)(2,1)S(1)} %get-tuple-element.8.refs_0_, bf16[1,32,2,32,128]{4,3,2,1,0:T(8,128)(2,1)S(1)} %get-tuple-element.9.refs_1_, ...), custom_call_target="tpu_custom_call" | custom-call | tf_op jit(solution)/shard_map/store_results/pallas_call | solution.py:328

commit v3 on v2

--- a/solution.py
+++ b/solution.py
@@ -20,8 +20,7 @@
 NT = (((1,), (1,)), ((), ()))
 NN = (((1,), (0,)), ((), ()))
 MESH = pl.DeviceIdType.MESH
-IN_GROUPS = ((0, 2), (2, 1), (3, 1))
-OUT_GROUPS = ((0, 1), (1, 1), (2, 2))
+FAR_FIRST = ((4,), (3, 5), (2, 6), (1, 7))
 
 
 def dot(a, b, dims=NN):
@@ -83,7 +82,7 @@
         row_dot[:, tile(i)] = dot(ones, high, NT) + dot(ones, low, NT)
 
 
-def score_grads(weights, q, k_t, v, g, row_dot, ds, dq, dk):
+def score_grads(weights, k_t, v, g, row_dot, ds, dq):
     for i in range(NB):
         r = row_dot[0:1, tile(i)]
         for j in range(i + 1):
@@ -92,6 +91,9 @@
             ds[tile(j), tile(i)] = (w * (dp - r)).astype(jnp.bfloat16)
         grad = dot(k_t[:, 0 : (i + 1) * TB], ds[0 : (i + 1) * TB, tile(i)])
         dq[tile(i)] = (grad * SCALE).T.astype(jnp.bfloat16)
+
+
+def key_grads(ds, q, dk):
     for j in range(NB):
         n = NB - j
         dk[tile(j)] = (dot(ds[tile(j), tile(j, n)], q[tile(j, n)]) * SCALE).astype(jnp.bfloat16)
@@ -101,36 +103,56 @@
     q_in, k_in, v_in, g_in, o_out, dq_out, dk_out, dv_out,
     held, sent, items, made, given,
     scores, weights, ds, v_t, k_t, out_wide, row_dot,
-    load_sem, store_sem, in_send, in_recv, out_send, out_recv, own_send,
+    load_sem, in_send, in_recv, out_send, out_recv, own_send, ring_sem,
 ):
     seq = lax.axis_index("seq")
     ctx = lax.axis_index("ctx")
     head = lax.axis_index("head")
     me = seq * 32 + head
     z = head // 4
-    y = ((head // 2) % 2) * 2 + seq
+    high = (head // 2) % 2
+    y = high * 2 + seq
     core = head % 2
-    shifted_me = head >= H // 2
-    local = jnp.logical_or(jnp.logical_not(shifted_me), seq == 1)
-
-    def partner(t):
-        e = t // 8
-        z2 = (z + 3 * t) % 8
+    def device(seq2, plane, z2, high2, core2):
+        return seq2, plane, z2 * 4 + high2 * 2 + core2
+
+
+    def index_of(seq2, z2, high2, core2):
+        return seq2 * H + core2 * (H // 2) + z2 * 2 + high2
+
+    def neighbour(e):
         y2 = (y + e) % 4
-        core2 = (core + e // 4) % 2
-        return y2 % 2, z2 * 4 + (y2 // 2) * 2 + core2
-
-    def item_at(t):
-        seq2, head2 = partner(t)
-        shifted = (head2 >= H // 2).astype(jnp.int32)
-        plane = (ctx + 4 - shifted * (1 - seq)) % 4
-        return seq2, head2, plane, (me + 32 * shifted) % BLOCKS
-
-    def owner_at(t):
-        seq2, head2 = partner(t)
-        shifted = shifted_me.astype(jnp.int32)
-        plane = (ctx + shifted * (1 - seq2)) % 4
-        return seq2, head2, plane, (seq2 * 32 + head2 + 32 * shifted) % BLOCKS
+        return y2 % 2, y2 // 2, (core + e // 4) % 2
+
+    def each_partner(visit):
+        for distances in FAR_FIRST:
+            starts = [(z + dz) % 8 for dz in distances]
+
+            def step(e, carry, starts=starts):
+                seq2, high2, core2 = neighbour(e)
+                for z2 in starts:
+                    visit(seq2, z2, high2, core2)
+                return carry
+
+            lax.fori_loop(0, 8, step, 0)
+
+        def near(e, carry):
+            seq2, high2, core2 = neighbour(e)
+            visit(seq2, z, high2, core2)
+            return carry
+
+        lax.fori_loop(1, 8, near, 0)
+
+    def item_at(seq2, z2, high2, core2):
+        return (ctx + 4 - core2 * (1 - seq)) % 4, (me + 32 * core2) % BLOCKS
+
+    def owner_at(seq2, z2, high2, core2):
+        block = seq2 * 32 + z2 * 4 + high2 * 2 + core2
+        return (ctx + core * (1 - seq2)) % 4, (block + 32 * core) % BLOCKS
+
+    mine = index_of(seq, z, high, core)
+    local = core * (1 - seq) == 0
+    here = (seq, z, high, core)
 
     inputs = (q_in, k_in, v_in, g_in)
     loads = [
@@ -140,17 +162,32 @@
         load.start()
 
     barrier = pltpu.get_barrier_semaphore()
-
-    def greet(t, _):
-        seq2, head2, plane, _ = owner_at(t)
-        pl.semaphore_signal(barrier, inc=1, device_id=(seq2, plane, head2), device_id_type=MESH)
-        return _
-
-    lax.fori_loop(1, BLOCKS, greet, 0)
+    ring = [device(seq, ctx, (z + dz) % 8, high, core) for dz in range(1, 8)]
+
+    def greet(seq2, high2, core2):
+        plane, _ = owner_at(seq2, z, high2, core2)
+        pl.semaphore_signal(
+            barrier, inc=1, device_id=device(seq2, plane, z, high2, core2), device_id_type=MESH
+        )
+
+    def greet_neighbour(e, carry):
+        greet(*neighbour(e))
+        return carry
+
+    lax.fori_loop(1, 8, greet_neighbour, 0)
 
     @pl.when(jnp.logical_not(local))
     def _():
-        greet(0, 0)
+        greet(seq, high, core)
+
+    for to in ring:
+        pl.semaphore_signal(barrier, inc=1, device_id=to, device_id_type=MESH)
+
+    def all_in():
+        pl.semaphore_wait(barrier, 15 - local.astype(jnp.int32))
+        for to in ring:
+            pl.semaphore_signal(ring_sem, inc=1, device_id=to, device_id_type=MESH)
+        pl.semaphore_wait(ring_sem, 7)
 
     def by_head(a):
         loads[a].wait()
@@ -158,119 +195,102 @@
         sent[a] = jnp.swapaxes(x, 0, 1).reshape(T, D)
 
     def send_in(n):
-        first, count = IN_GROUPS[n]
-        slots = pl.ds(first, count)
-
-        def copy(t, send_sem):
-            seq2, head2, plane, place = item_at(t)
+        def copy(at, send_sem):
+            plane, place = item_at(*at)
             return pltpu.make_async_remote_copy(
-                src_ref=sent.at[slots, rows(seq2 * 32 + head2)],
-                dst_ref=items.at[slots, rows(place)],
+                src_ref=sent.at[n, rows(index_of(*at))],
+                dst_ref=items.at[n, rows(place)],
                 send_sem=send_sem,
                 recv_sem=in_recv.at[n],
-                device_id=(seq2, plane, head2),
+                device_id=device(at[0], plane, *at[1:]),
                 device_id_type=MESH,
             )
 
+        each_partner(lambda *at: copy(at, in_send.at[n]).start())
+
         @pl.when(local)
         def _():
-            place = (me + 32 * shifted_me.astype(jnp.int32)) % BLOCKS
+            _, place = item_at(*here)
             pltpu.make_async_copy(
-                sent.at[slots, rows(me)], items.at[slots, rows(place)], in_recv.at[n]
+                sent.at[n, rows(mine)], items.at[n, rows(place)], in_recv.at[n]
             ).start()
 
         @pl.when(jnp.logical_not(local))
         def _():
-            copy(0, own_send.at[n]).start()
-
-        def step(t, _):
-            copy(t, in_send.at[n]).start()
-            return _
-
-        lax.fori_loop(1, BLOCKS, step, 0)
+            copy(here, own_send.at[n]).start()
 
     def send_out(n):
-        first, count = OUT_GROUPS[n]
-        slots = pl.ds(first, count)
-
-        def copy(t, send_sem):
-            seq2, head2, plane, place = owner_at(t)
+        def copy(at, send_sem):
+            plane, place = owner_at(*at)
             return pltpu.make_async_remote_copy(
-                src_ref=made.at[slots, rows(place)],
-                dst_ref=given.at[slots, rows(me)],
+                src_ref=made.at[n, rows(place)],
+                dst_ref=given.at[n, rows(mine)],
                 send_sem=send_sem,
                 recv_sem=out_recv.at[n],
-                device_id=(seq2, plane, head2),
+                device_id=device(at[0], plane, *at[1:]),
                 device_id_type=MESH,
             )
 
+        each_partner(lambda *at: copy(at, out_send.at[n]).start())
+
         @pl.when(local)
         def _():
-            place = (me + 32 * shifted_me.astype(jnp.int32)) % BLOCKS
+            _, place = owner_at(*here)
             pltpu.make_async_copy(
-                made.at[slots, rows(place)], given.at[slots, rows(me)], out_recv.at[n]
+                made.at[n, rows(place)], given.at[n, rows(mine)], out_recv.at[n]
             ).start()
 
         @pl.when(jnp.logical_not(local))
         def _():
-            copy(0, own_send.at[3 + n]).start()
-
-        def step(t, _):
-            copy(t, out_send.at[n]).start()
-            return _
-
-        lax.fori_loop(1, BLOCKS, step, 0)
-
-    def arrived(buffer, groups, sems, n):
-        first, count = groups[n]
-        whole = buffer.at[pl.ds(first, count)]
-        pltpu.make_async_copy(whole, whole, sems.at[n]).wait()
-
-    def left(buffer, groups, sems, n, own):
-        first, count = groups[n]
-        most = buffer.at[pl.ds(first, count), pl.ds(0, T - ROWS)]
+            copy(here, own_send.at[4 + n]).start()
+
+    def arrived(buffer, sems, n):
+        pltpu.make_async_copy(buffer.at[n], buffer.at[n], sems.at[n]).wait()
+
+    def left(buffer, sems, n, own):
+        most = buffer.at[n, pl.ds(0, T - ROWS)]
         pltpu.make_async_copy(most, most, sems.at[n]).wait()
 
         @pl.when(jnp.logical_not(local))
         def _():
-            one = buffer.at[pl.ds(first, count), pl.ds(0, ROWS)]
+            one = buffer.at[n, pl.ds(0, ROWS)]
             pltpu.make_async_copy(one, one, own_send.at[own]).wait()
 
-    by_head(0)
-    by_head(1)
-    pl.semaphore_wait(barrier, BLOCKS - local.astype(jnp.int32))
-    send_in(0)
-    by_head(2)
-    send_in(1)
-    by_head(3)
-    send_in(2)
+    for n in range(4):
+        by_head(n)
+        if n == 0:
+            all_in()
+        send_in(n)
 
     q, k, v, g = (items.at[a] for a in range(4))
-    arrived(items, IN_GROUPS, in_recv, 0)
+    o, dv, dq, dk = (made.at[a] for a in range(4))
+    arrived(items, in_recv, 0)
+    arrived(items, in_recv, 1)
     softmax_weights(q, k, scores, weights)
     k_t[...] = k[...].T
-    arrived(items, IN_GROUPS, in_recv, 1)
+    arrived(items, in_recv, 2)
     v_t[...] = v[...].T
-    attended(v_t, weights, made.at[0], out_wide)
+    attended(v_t, weights, o, out_wide)
     send_out(0)
-    arrived(items, IN_GROUPS, in_recv, 2)
-    value_grads(weights, g, made.at[1])
+    arrived(items, in_recv, 3)
+    value_grads(weights, g, dv)
     send_out(1)
     row_dots(g, out_wide, row_dot)
-    score_grads(weights, q, k_t, v, g, row_dot, ds, made.at[2], made.at[3])
+    score_grads(weights, k_t, v, g, row_dot, ds, dq)
     send_out(2)
-
-    for n in range(3):
-        left(sent, IN_GROUPS, in_send, n, n)
+    key_grads(ds, q, dk)
+    send_out(3)
+
+    for n in range(4):
+        left(sent, in_send, n, n)
 
     outputs = (o_out, dv_out, dq_out, dk_out)
-    for n, (first, count) in enumerate(OUT_GROUPS):
-        arrived(given, OUT_GROUPS, out_recv, n)
-        for a in range(first, first + count):
-            x = given[a].reshape(BLOCKS, ROWS, D)
-            outputs[a][0] = jnp.swapaxes(x, 0, 1).reshape(ROWS, 2, H, D)
-    for n in range(3):
-        left(made, OUT_GROUPS, out_send, n, 3 + n)
+    for n in range(4):
+        arrived(given, out_recv, n)
+        x = given[n].reshape(BLOCKS, ROWS, D)
+        outputs[n][0] = jnp.swapaxes(x, 0, 1).reshape(ROWS, 2, H, D)
+    for n in range(4):
+        left(made, out_send, n, 4 + n)
 
 
 def store_results(*refs):
@@ -307,11 +327,11 @@
             pltpu.VMEM((8, T), wide),
             pltpu.SemaphoreType.DMA((4,)),
             pltpu.SemaphoreType.DMA((4,)),
-            pltpu.SemaphoreType.DMA((3,)),
-            pltpu.SemaphoreType.DMA((3,)),
-            pltpu.SemaphoreType.DMA((3,)),
-            pltpu.SemaphoreType.DMA((3,)),
-            pltpu.SemaphoreType.DMA((6,)),
+            pltpu.SemaphoreType.DMA((4,)),
+            pltpu.SemaphoreType.DMA((4,)),
+            pltpu.SemaphoreType.DMA((4,)),
+            pltpu.SemaphoreType.DMA((8,)),
+            pltpu.SemaphoreType.REGULAR,
         ],
         compiler_params=pltpu.CompilerParams(
             collective_id=0, has_side_effects=True, vmem_limit_bytes=36 << 20

time: 110 us -> 109 us (level)
    pallas_call x1, Pallas kernels: 108 us -> 106 us  [shards(): pl.pallas_call(kernel, out_shape=[pltpu.VMEM(queries.shape, low)] * 4, in...]
where the time goes in v3:
time: 109 us; the launch traced here: 108 us
  Pallas kernels  108 us (99%)
    pallas_call x1, Pallas kernels, shards(): pl.pallas_call(kernel, out_shape=[pltpu.VMEM(queries.shape, low)] * 4, in...  106 us

profile of v3, /device:TPU:1, one launch (start us, length us, event | category | flops | bytes accessed | tf_op | source)
XLA Modules:
  0.0 108.4 jit_solution(3300225626517203155)
XLA Ops:
  0.6 106.3 %shifted_attention.1 = (bf16[1,32,2,32,128]{4,3,2,1,0:T(8,128)(2,1)S(1)}, bf16[1,32,2,32,128]{4,3,2,1,0:T(8,128)(2,1)S(1)}, bf16[1,32,2,32,128]{4,3,2,1,0:T(8,128)(2,1)S(1)}, bf16[1,32,2,32,128]{4,3,2,1,0:T(8,128)(2,1)S(1)}) custom-call(bf16[1,32,2,32,128]{4,3,2,1,0:T(8,128)(2,1)} %q_in.1, bf16[1,32,2,32,128]{4,3,2,1,0:T(8,128)(2,1)} %k_in.1, ...), custom_call_target="tpu_custom_call" | custom-call | flops 3221225472 | bytes 4194304 | tf_op jit(solution)/shard_map/shifted_attention/pallas_call | solution.py:310
  106.9 1.3 %store_results.1 = (bf16[1,32,2,32,128]{4,3,2,1,0:T(8,128)(2,1)}, bf16[1,32,2,32,128]{4,3,2,1,0:T(8,128)(2,1)}, bf16[1,32,2,32,128]{4,3,2,1,0:T(8,128)(2,1)}, bf16[1,32,2,32,128]{4,3,2,1,0:T(8,128)(2,1)}) custom-call(bf16[1,32,2,32,128]{4,3,2,1,0:T(8,128)(2,1)S(1)} %get-tuple-element.8.refs_0_, bf16[1,32,2,32,128]{4,3,2,1,0:T(8,128)(2,1)S(1)} %get-tuple-element.9.refs_1_, ...), custom_call_target="tpu_custom_call" | custom-call | tf_op jit(solution)/shard_map/store_results/pallas_call | solution.py:348

commit v4 on v3

--- a/solution.py
+++ b/solution.py
@@ -20,7 +20,7 @@
 NT = (((1,), (1,)), ((), ()))
 NN = (((1,), (0,)), ((), ()))
 MESH = pl.DeviceIdType.MESH
-FAR_FIRST = ((4,), (3, 5), (2, 6), (1, 7))
+DISTANCES = (4, 0, 3, 5, 2, 6, 1, 7)
 
 
 def dot(a, b, dims=NN):
@@ -103,7 +103,7 @@
     q_in, k_in, v_in, g_in, o_out, dq_out, dk_out, dv_out,
     held, sent, items, made, given,
     scores, weights, ds, v_t, k_t, out_wide, row_dot,
-    load_sem, in_send, in_recv, out_send, out_recv, own_send, ring_sem,
+    load_sem, in_send, in_recv, out_send, out_recv, own_send,
 ):
     seq = lax.axis_index("seq")
     ctx = lax.axis_index("ctx")
@@ -113,6 +113,7 @@
     high = (head // 2) % 2
     y = high * 2 + seq
     core = head % 2
+
     def device(seq2, plane, z2, high2, core2):
         return seq2, plane, z2 * 4 + high2 * 2 + core2
 
@@ -125,23 +126,18 @@
         return y2 % 2, y2 // 2, (core + e // 4) % 2
 
     def each_partner(visit):
-        for distances in FAR_FIRST:
-            starts = [(z + dz) % 8 for dz in distances]
-
-            def step(e, carry, starts=starts):
-                seq2, high2, core2 = neighbour(e)
-                for z2 in starts:
-                    visit(seq2, z2, high2, core2)
-                return carry
-
-            lax.fori_loop(0, 8, step, 0)
-
-        def near(e, carry):
+        starts = [(z + dz) % 8 for dz in DISTANCES]
+        for dz, z2 in zip(DISTANCES, starts):
+            if dz:
+                visit(seq, z2, high, core)
+
+        def step(e, carry):
             seq2, high2, core2 = neighbour(e)
-            visit(seq2, z, high2, core2)
+            for z2 in starts:
+                visit(seq2, z2, high2, core2)
             return carry
 
-        lax.fori_loop(1, 8, near, 0)
+        lax.fori_loop(1, 8, step, 0)
 
     def item_at(seq2, z2, high2, core2):
         return (ctx + 4 - core2 * (1 - seq)) % 4, (me + 32 * core2) % BLOCKS
@@ -153,6 +149,24 @@
     mine = index_of(seq, z, high, core)
     local = core * (1 - seq) == 0
     here = (seq, z, high, core)
+
+    barrier = pltpu.get_barrier_semaphore()
+
+    def greet(*at):
+        plane, _ = owner_at(*at)
+        pl.semaphore_signal(
+            barrier, inc=1, device_id=device(at[0], plane, *at[1:]), device_id_type=MESH
+        )
+
+    for e in range(8):
+        seq2, high2, core2 = neighbour(e)
+        for dz in DISTANCES:
+            if (e, dz) != (0, 0):
+                greet(seq2, (z + dz) % 8, high2, core2)
+
+    @pl.when(jnp.logical_not(local))
+    def _():
+        greet(*here)
 
     inputs = (q_in, k_in, v_in, g_in)
     loads = [
@@ -160,34 +174,6 @@
     ]
     for load in loads:
         load.start()
-
-    barrier = pltpu.get_barrier_semaphore()
-    ring = [device(seq, ctx, (z + dz) % 8, high, core) for dz in range(1, 8)]
-
-    def greet(seq2, high2, core2):
-        plane, _ = owner_at(seq2, z, high2, core2)
-        pl.semaphore_signal(
-            barrier, inc=1, device_id=device(seq2, plane, z, high2, core2), device_id_type=MESH
-        )
-
-    def greet_neighbour(e, carry):
-        greet(*neighbour(e))
-        return carry
-
-    lax.fori_loop(1, 8, greet_neighbour, 0)
-
-    @pl.when(jnp.logical_not(local))
-    def _():
-        greet(seq, high, core)
-
-    for to in ring:
-        pl.semaphore_signal(barrier, inc=1, device_id=to, device_id_type=MESH)
-
-    def all_in():
-        pl.semaphore_wait(barrier, 15 - local.astype(jnp.int32))
-        for to in ring:
-            pl.semaphore_signal(ring_sem, inc=1, device_id=to, device_id_type=MESH)
-        pl.semaphore_wait(ring_sem, 7)
 
     def by_head(a):
         loads[a].wait()
@@ -259,7 +245,7 @@
     for n in range(4):
         by_head(n)
         if n == 0:
-            all_in()
+            pl.semaphore_wait(barrier, BLOCKS - local.astype(jnp.int32))
         send_in(n)
 
     q, k, v, g = (items.at[a] for a in range(4))
@@ -331,7 +317,6 @@
             pltpu.SemaphoreType.DMA((4,)),
             pltpu.SemaphoreType.DMA((4,)),
             pltpu.SemaphoreType.DMA((8,)),
-            pltpu.SemaphoreType.REGULAR,
         ],
         compiler_params=pltpu.CompilerParams(
             collective_id=0, has_side_effects=True, vmem_limit_bytes=36 << 20

time: 109 us -> 107 us (0.982)
  no operation moved by 1% of the time
where the time goes in v4:
time: 107 us
  Pallas kernels  107 us (100%)
    pallas_call x1, Pallas kernels, shards(): pl.pallas_call(kernel, out_shape=[pltpu.VMEM(queries.shape, low)] * 4, in...  105 us

profile of v4, /device:TPU:1, one launch (start us, length us, event | category | flops | bytes accessed | tf_op | source)
XLA Modules:
  0.0 107.4 jit_solution(11127520706276370081)
XLA Ops:
  0.6 105.4 %shifted_attention.1 = (bf16[1,32,2,32,128]{4,3,2,1,0:T(8,128)(2,1)S(1)}, bf16[1,32,2,32,128]{4,3,2,1,0:T(8,128)(2,1)S(1)}, bf16[1,32,2,32,128]{4,3,2,1,0:T(8,128)(2,1)S(1)}, bf16[1,32,2,32,128]{4,3,2,1,0:T(8,128)(2,1)S(1)}) custom-call(bf16[1,32,2,32,128]{4,3,2,1,0:T(8,128)(2,1)} %q_in.1, bf16[1,32,2,32,128]{4,3,2,1,0:T(8,128)(2,1)} %k_in.1, ...), custom_call_target="tpu_custom_call" | custom-call | flops 3221225472 | bytes 4194304 | tf_op jit(solution)/shard_map/shifted_attention/pallas_call | solution.py:296
  106.0 1.3 %store_results.1 = (bf16[1,32,2,32,128]{4,3,2,1,0:T(8,128)(2,1)}, bf16[1,32,2,32,128]{4,3,2,1,0:T(8,128)(2,1)}, bf16[1,32,2,32,128]{4,3,2,1,0:T(8,128)(2,1)}, bf16[1,32,2,32,128]{4,3,2,1,0:T(8,128)(2,1)}) custom-call(bf16[1,32,2,32,128]{4,3,2,1,0:T(8,128)(2,1)S(1)} %get-tuple-element.8.refs_0_, bf16[1,32,2,32,128]{4,3,2,1,0:T(8,128)(2,1)S(1)} %get-tuple-element.9.refs_1_, ...), custom_call_target="tpu_custom_call" | custom-call | tf_op jit(solution)/shard_map/store_results/pallas_call | solution.py:333

commit v5 on v4

--- a/solution.py
+++ b/solution.py
@@ -122,14 +122,11 @@
         return seq2 * H + core2 * (H // 2) + z2 * 2 + high2
 
     def neighbour(e):
-        y2 = (y + e) % 4
-        return y2 % 2, y2 // 2, (core + e // 4) % 2
+        y2 = (y + e + 1) % 4
+        return y2 % 2, y2 // 2, (core + 1 + e // 4) % 2
 
     def each_partner(visit):
         starts = [(z + dz) % 8 for dz in DISTANCES]
-        for dz, z2 in zip(DISTANCES, starts):
-            if dz:
-                visit(seq, z2, high, core)
 
         def step(e, carry):
             seq2, high2, core2 = neighbour(e)
@@ -137,7 +134,10 @@
                 visit(seq2, z2, high2, core2)
             return carry
 
-        lax.fori_loop(1, 8, step, 0)
+        lax.fori_loop(0, 7, step, 0)
+        for dz, z2 in zip(DISTANCES, starts):
+            if dz:
+                visit(seq, z2, high, core)
 
     def item_at(seq2, z2, high2, core2):
         return (ctx + 4 - core2 * (1 - seq)) % 4, (me + 32 * core2) % BLOCKS
@@ -161,7 +161,7 @@
     for e in range(8):
         seq2, high2, core2 = neighbour(e)
         for dz in DISTANCES:
-            if (e, dz) != (0, 0):
+            if (e, dz) != (7, 0):
                 greet(seq2, (z + dz) % 8, high2, core2)
 
     @pl.when(jnp.logical_not(local))

time: 107 us -> 107 us (level)
  no operation moved by 1% of the time
where the time goes in v5:
time: 107 us
  Pallas kernels  106 us (99%)
    pallas_call x1, Pallas kernels, shards(): pl.pallas_call(kernel, out_shape=[pltpu.VMEM(queries.shape, low)] * 4, in...  105 us

profile of v5, /device:TPU:1, one launch (start us, length us, event | category | flops | bytes accessed | tf_op | source)
XLA Modules:
  0.0 107.0 jit_solution(16727603244015691044)
XLA Ops:
  0.6 104.8 %shifted_attention.1 = (bf16[1,32,2,32,128]{4,3,2,1,0:T(8,128)(2,1)S(1)}, bf16[1,32,2,32,128]{4,3,2,1,0:T(8,128)(2,1)S(1)}, bf16[1,32,2,32,128]{4,3,2,1,0:T(8,128)(2,1)S(1)}, bf16[1,32,2,32,128]{4,3,2,1,0:T(8,128)(2,1)S(1)}) custom-call(bf16[1,32,2,32,128]{4,3,2,1,0:T(8,128)(2,1)} %q_in.1, bf16[1,32,2,32,128]{4,3,2,1,0:T(8,128)(2,1)} %k_in.1, ...), custom_call_target="tpu_custom_call" | custom-call | flops 3221225472 | bytes 4194304 | tf_op jit(solution)/shard_map/shifted_attention/pallas_call | solution.py:296
  105.4 1.3 %store_results.1 = (bf16[1,32,2,32,128]{4,3,2,1,0:T(8,128)(2,1)}, bf16[1,32,2,32,128]{4,3,2,1,0:T(8,128)(2,1)}, bf16[1,32,2,32,128]{4,3,2,1,0:T(8,128)(2,1)}, bf16[1,32,2,32,128]{4,3,2,1,0:T(8,128)(2,1)}) custom-call(bf16[1,32,2,32,128]{4,3,2,1,0:T(8,128)(2,1)S(1)} %get-tuple-element.8.refs_0_, bf16[1,32,2,32,128]{4,3,2,1,0:T(8,128)(2,1)S(1)} %get-tuple-element.9.refs_1_, ...), custom_call_target="tpu_custom_call" | custom-call | tf_op jit(solution)/shard_map/store_results/pallas_call | solution.py:333

commit v6 on v5

--- a/solution.py
+++ b/solution.py
@@ -21,6 +21,12 @@
 NN = (((1,), (0,)), ((), ()))
 MESH = pl.DeviceIdType.MESH
 DISTANCES = (4, 0, 3, 5, 2, 6, 1, 7)
+
+
+FAR_TO_NEAR = sorted(
+    ((e, dz) for e in range(8) for dz in DISTANCES if (e, dz) != (7, 0)),
+    key=lambda at: -min(at[1], 8 - at[1]) - (1, 2, 1, 0)[at[0] % 4],
+)
 
 
 def dot(a, b, dims=NN):
@@ -158,11 +164,9 @@
             barrier, inc=1, device_id=device(at[0], plane, *at[1:]), device_id_type=MESH
         )
 
-    for e in range(8):
+    for e, dz in FAR_TO_NEAR:
         seq2, high2, core2 = neighbour(e)
-        for dz in DISTANCES:
-            if (e, dz) != (7, 0):
-                greet(seq2, (z + dz) % 8, high2, core2)
+        greet(seq2, (z + dz) % 8, high2, core2)
 
     @pl.when(jnp.logical_not(local))
     def _():

time: 107 us -> 107 us (level)
  no operation moved by 1% of the time
where the time goes in v6:
time: 107 us
  Pallas kernels  106 us (99%)
    pallas_call x1, Pallas kernels, shards(): pl.pallas_call(kernel, out_shape=[pltpu.VMEM(queries.shape, low)] * 4, in...  105 us

profile of v6, /device:TPU:1, one launch (start us, length us, event | category | flops | bytes accessed | tf_op | source)
XLA Modules:
  0.0 107.2 jit_solution(3032725506608871053)
XLA Ops:
  0.6 105.1 %shifted_attention.1 = (bf16[1,32,2,32,128]{4,3,2,1,0:T(8,128)(2,1)S(1)}, bf16[1,32,2,32,128]{4,3,2,1,0:T(8,128)(2,1)S(1)}, bf16[1,32,2,32,128]{4,3,2,1,0:T(8,128)(2,1)S(1)}, bf16[1,32,2,32,128]{4,3,2,1,0:T(8,128)(2,1)S(1)}) custom-call(bf16[1,32,2,32,128]{4,3,2,1,0:T(8,128)(2,1)} %q_in.1, bf16[1,32,2,32,128]{4,3,2,1,0:T(8,128)(2,1)} %k_in.1, ...), custom_call_target="tpu_custom_call" | custom-call | flops 3221225472 | bytes 4194304 | tf_op jit(solution)/shard_map/shifted_attention/pallas_call | solution.py:300
  105.7 1.3 %store_results.1 = (bf16[1,32,2,32,128]{4,3,2,1,0:T(8,128)(2,1)}, bf16[1,32,2,32,128]{4,3,2,1,0:T(8,128)(2,1)}, bf16[1,32,2,32,128]{4,3,2,1,0:T(8,128)(2,1)}, bf16[1,32,2,32,128]{4,3,2,1,0:T(8,128)(2,1)}) custom-call(bf16[1,32,2,32,128]{4,3,2,1,0:T(8,128)(2,1)S(1)} %get-tuple-element.8.refs_0_, bf16[1,32,2,32,128]{4,3,2,1,0:T(8,128)(2,1)S(1)} %get-tuple-element.9.refs_1_, ...), custom_call_target="tpu_custom_call" | custom-call | tf_op jit(solution)/shard_map/store_results/pallas_call | solution.py:337

commit v7 on v5

--- a/solution.py
+++ b/solution.py
@@ -99,8 +99,12 @@
         dk[tile(j)] = (dot(ds[tile(j), tile(j, n)], q[tile(j, n)]) * SCALE).astype(jnp.bfloat16)
 
 
+def by_position(x):
+    return jnp.swapaxes(x.reshape(BLOCKS, ROWS, D), 0, 1).reshape(ROWS, 2, H, D)
+
+
 def kernel(
-    q_in, k_in, v_in, g_in, o_out, dq_out, dk_out, dv_out,
+    q_in, k_in, v_in, g_in, o_out, dq_out, dk_raw, dv_out,
     held, sent, items, made, given,
     scores, weights, ds, v_t, k_t, out_wide, row_dot,
     load_sem, in_send, in_recv, out_send, out_recv, own_send,
@@ -205,12 +209,15 @@
         def _():
             copy(here, own_send.at[n]).start()
 
+    def landing(n):
+        return dk_raw if n == 3 else given.at[n]
+
     def send_out(n):
         def copy(at, send_sem):
             plane, place = owner_at(*at)
             return pltpu.make_async_remote_copy(
                 src_ref=made.at[n, rows(place)],
-                dst_ref=given.at[n, rows(mine)],
+                dst_ref=landing(n).at[rows(mine)],
                 send_sem=send_sem,
                 recv_sem=out_recv.at[n],
                 device_id=device(at[0], plane, *at[1:]),
@@ -223,15 +230,15 @@
         def _():
             _, place = owner_at(*here)
             pltpu.make_async_copy(
-                made.at[n, rows(place)], given.at[n, rows(mine)], out_recv.at[n]
+                made.at[n, rows(place)], landing(n).at[rows(mine)], out_recv.at[n]
             ).start()
 
         @pl.when(jnp.logical_not(local))
         def _():
             copy(here, own_send.at[4 + n]).start()
 
-    def arrived(buffer, sems, n):
-        pltpu.make_async_copy(buffer.at[n], buffer.at[n], sems.at[n]).wait()
+    def arrived(whole, sem):
+        pltpu.make_async_copy(whole, whole, sem).wait()
 
     def left(buffer, sems, n, own):
         most = buffer.at[n, pl.ds(0, T - ROWS)]
@@ -250,15 +257,15 @@
 
     q, k, v, g = (items.at[a] for a in range(4))
     o, dv, dq, dk = (made.at[a] for a in range(4))
-    arrived(items, in_recv, 0)
-    arrived(items, in_recv, 1)
+    arrived(items.at[0], in_recv.at[0])
+    arrived(items.at[1], in_recv.at[1])
     softmax_weights(q, k, scores, weights)
     k_t[...] = k[...].T
-    arrived(items, in_recv, 2)
+    arrived(items.at[2], in_recv.at[2])
     v_t[...] = v[...].T
     attended(v_t, weights, o, out_wide)
     send_out(0)
-    arrived(items, in_recv, 3)
+    arrived(items.at[3], in_recv.at[3])
     value_grads(weights, g, dv)
     send_out(1)
     row_dots(g, out_wide, row_dot)
@@ -270,20 +277,25 @@
     for n in range(4):
         left(sent, in_send, n, n)
 
-    outputs = (o_out, dv_out, dq_out, dk_out)
+    outputs = (o_out, dv_out, dq_out)
     for n in range(4):
-        arrived(given, out_recv, n)
-        x = given[n].reshape(BLOCKS, ROWS, D)
-        outputs[n][0] = jnp.swapaxes(x, 0, 1).reshape(ROWS, 2, H, D)
+        arrived(landing(n), out_recv.at[n])
+        if n < 3:
+            outputs[n][0] = by_position(given[n])
     for n in range(4):
         left(made, out_send, n, 4 + n)
 
 
-def store_results(*refs):
-    sems = refs[8]
-    copies = [pltpu.make_async_copy(refs[a], refs[4 + a], sems.at[a]) for a in range(4)]
-    for copy in copies:
+def store_results(o, dq, dk_raw, dv, o_out, dq_out, dk_out, dv_out, dk, sems):
+    pairs = ((o, o_out.at[0]), (dq, dq_out.at[0]), (dv, dv_out.at[0]), (dk, dk_out.at[0]))
+    copies = [
+        pltpu.make_async_copy(src if n == 3 else src.at[0], dst, sems.at[n])
+        for n, (src, dst) in enumerate(pairs)
+    ]
+    for copy in copies[:3]:
         copy.start()
+    dk[...] = by_position(dk_raw[...])
+    copies[3].start()
     for copy in copies:
         copy.wait()
 
@@ -295,7 +307,7 @@
     low, wide = jnp.bfloat16, jnp.float32
     results = pl.pallas_call(
         kernel,
-        out_shape=[pltpu.VMEM(queries.shape, low)] * 4,
+        out_shape=[pltpu.VMEM(s, low) for s in (block.shape, block.shape, (T, D), block.shape)],
         in_specs=[in_hbm] * 4,
         out_specs=[in_vmem] * 4,
         scratch_shapes=[
@@ -303,7 +315,7 @@
             pltpu.VMEM((4, T, D), low),
             pltpu.VMEM((4, T, D), low),
             pltpu.VMEM((4, T, D), low),
-            pltpu.VMEM((4, T, D), low),
+            pltpu.VMEM((3, T, D), low),
             pltpu.VMEM((T, TB), wide),
             pltpu.VMEM((T, T), low),
             pltpu.VMEM((T, T), low),
@@ -335,7 +347,7 @@
             out_shape=[block] * 4,
             in_specs=[in_vmem] * 4,
             out_specs=[in_hbm] * 4,
-            scratch_shapes=[pltpu.SemaphoreType.DMA((4,))],
+            scratch_shapes=[pltpu.VMEM((ROWS, 2, H, D), low), pltpu.SemaphoreType.DMA((4,))],
             compiler_params=pltpu.CompilerParams(vmem_limit_bytes=4 << 20),
             name="store_results",
         )(*[pltpu.with_memory_space_constraint(x, pltpu.VMEM) for x in results])

time: 107 us -> 107 us (level)
  no operation moved by 1% of the time
where the time goes in v7:
time: 107 us
  Pallas kernels  106 us (99%)
    pallas_call x1, Pallas kernels, shards(): pl.pallas_call(kernel, out_shape=[pltpu.VMEM(s, low) for s in (block.shap...  105 us

profile of v7, /device:TPU:1, one launch (start us, length us, event | category | flops | bytes accessed | tf_op | source)
XLA Modules:
  0.0 106.8 jit_solution(7569651750677563875)
XLA Ops:
  0.6 104.6 %shifted_attention.1 = (bf16[1,32,2,32,128]{4,3,2,1,0:T(8,128)(2,1)S(1)}, bf16[1,32,2,32,128]{4,3,2,1,0:T(8,128)(2,1)S(1)}, bf16[2048,128]{1,0:T(8,128)(2,1)S(1)}, bf16[1,32,2,32,128]{4,3,2,1,0:T(8,128)(2,1)S(1)}) custom-call(bf16[1,32,2,32,128]{4,3,2,1,0:T(8,128)(2,1)} %q_in.1, bf16[1,32,2,32,128]{4,3,2,1,0:T(8,128)(2,1)} %k_in.1, ...), custom_call_target="tpu_custom_call" | custom-call | flops 3221225472 | bytes 4194304 | tf_op jit(solution)/shard_map/shifted_attention/pallas_call | solution.py:308
  105.3 1.3 %store_results.1 = (bf16[1,32,2,32,128]{4,3,2,1,0:T(8,128)(2,1)}, bf16[1,32,2,32,128]{4,3,2,1,0:T(8,128)(2,1)}, bf16[1,32,2,32,128]{4,3,2,1,0:T(8,128)(2,1)}, bf16[1,32,2,32,128]{4,3,2,1,0:T(8,128)(2,1)}) custom-call(bf16[1,32,2,32,128]{4,3,2,1,0:T(8,128)(2,1)S(1)} %get-tuple-element.8.o, bf16[1,32,2,32,128]{4,3,2,1,0:T(8,128)(2,1)S(1)} %get-tuple-element.9.dq, ...), custom_call_target="tpu_custom_call" | custom-call | tf_op jit(solution)/shard_map/store_results/pallas_call | solution.py:345
